TPU v7x, 256 devices: a whole 4x4x8 slice. The times are simulated.
256 devices in a mesh: fsdp: 32 (over y, x, core), ctx: 8 (over z).
Axes of the slice: x: 4, y: 4, z: 8, core: 2. Of those that a mesh axis runs over, the one named last changes fastest.
Arguments:
- tokens: bfloat16 [16384, 8192], P('fsdp'), may hold values from -12 to 12
- wq: bfloat16 [8192, 4096], P('fsdp', 'ctx'), may hold values from -0.0625 to 0.0625
- wo: bfloat16 [4096, 8192], P('ctx', 'fsdp'), may hold values from -1.5 to 1.5
- key_cache: bfloat16 [65536, 1024], P(('fsdp', 'ctx')), may hold values from -500 to 500, as said below
- value_cache: bfloat16 [65536, 1024], P(('fsdp', 'ctx')), may hold values from -6 to 6
- key_blocks: int32 [32, 4, 8], P('fsdp'), may hold values from 0 to 15, as said below
Outputs:
- mixed: bfloat16 [16384, 8192], P('fsdp', 'ctx')
Inputs may be any that keep to these rules, and one draw needn't show every extreme that they name: `key_cache`: keys of order one; a sequence's first block may hold much larger ones. `key_blocks`: for query block b of sequence s, entries 0 to 2 name key blocks 16 - 4 + b - 2, 12 + b - 1 and 12 + b; entries 3 and 4 name blocks 0 and 1; the last 3 entries are random blocks. Counting the random entries of a sequence over its query blocks in order as t = 0, 1, ..., the t-th lies in blocks k * 2 to (k+1) * 2 - 1 with k = 1 + t mod (6); entries may repeat.
All inputs are finite; a program needn't handle non-finite values.
Results may differ from a plain program's by a relative error of at most 0.018.
Values may be sent and summed in bfloat16 or wider, within the bound.
No kernel may reach another device: no remote copies, remote signals or barrier semaphores. Data moves between devices by JAX's collectives and lax.ppermute only.
A program may use at most 128 MiB of HBM per device.

v0:
```python
import jax
import jax.numpy as jnp
from jax import lax
from jax.sharding import PartitionSpec as P

HEAD = 128
BLOCK = 128
rope_base = 1000000.0


def rotate(vectors, positions):
    half_width = vectors.shape[-1] // 2
    frequency = rope_base ** (
        -(jnp.arange(half_width, dtype=jnp.float32) * 2.0) / vectors.shape[-1]
    )
    angles = positions.astype(jnp.float32)[:, None] * frequency[None, :]
    cosine_table = jnp.cos(angles)[:, None, :]
    sine_table = jnp.sin(angles)[:, None, :]
    front_half = vectors[..., :half_width]
    back_half = vectors[..., half_width:]
    return jnp.concatenate(
        [
            front_half * cosine_table - back_half * sine_table,
            back_half * cosine_table + front_half * sine_table,
        ],
        axis=-1,
    )


def body(tokens, wq, wo, key_cache, value_cache, key_blocks):
    ctx_count = lax.axis_size("ctx")
    row_count = tokens.shape[0]
    query_cols = wq.shape[1]
    projected = jnp.dot(
        tokens, lax.all_gather(wq, "fsdp", axis=0, tiled=True), preferred_element_type=jnp.float32
    )
    cache_count = key_cache.shape[0]
    key_total = cache_count * ctx_count
    positions = key_total - row_count + jnp.arange(row_count, dtype=jnp.int32)
    query = (
        rotate(projected.reshape(row_count, query_cols // HEAD, HEAD), positions) * HEAD ** (-0.5)
    ).astype(jnp.bfloat16)
    kv_cols = key_cache.shape[1] // ctx_count
    keys_whole, values_whole = (
        lax.all_gather(key_cache, "ctx", axis=0, tiled=True),
        lax.all_gather(value_cache, "ctx", axis=0, tiled=True),
    )
    first_col = lax.axis_index("ctx") * kv_cols
    keys_all = lax.dynamic_slice_in_dim(keys_whole, first_col, kv_cols, 1)
    values_all = lax.dynamic_slice_in_dim(values_whole, first_col, kv_cols, 1)
    kv_local = kv_cols // HEAD
    group_size = query_cols // kv_cols
    block_count = key_total // BLOCK
    query_blocks = row_count // BLOCK
    lists = key_blocks[0]
    picked_keys = jnp.take(keys_all.reshape(block_count, BLOCK, kv_local, HEAD), lists, axis=0)
    picked_values = jnp.take(values_all.reshape(block_count, BLOCK, kv_local, HEAD), lists, axis=0)
    shaped = query.reshape(query_blocks, BLOCK, kv_local, group_size, HEAD)
    scores = jnp.einsum(
        "bqkgd,bnskd->bkgqns", shaped, picked_keys, preferred_element_type=jnp.float32
    )
    own_block = block_count - query_blocks + jnp.arange(query_blocks, dtype=jnp.int32)
    own = lists == own_block[:, None]
    causal = jnp.arange(BLOCK)[None, :] <= jnp.arange(BLOCK)[:, None]
    allowed = jnp.logical_or(
        jnp.logical_not(own)[:, None, None, None, :, None], causal[None, None, None, :, None, :]
    )
    scores = jnp.where(allowed, scores, -jnp.inf)
    top_score = jnp.max(scores, axis=(4, 5), keepdims=True)
    raised = jnp.exp(scores - top_score)
    weights = (raised / jnp.sum(raised, axis=(4, 5), keepdims=True)).astype(jnp.bfloat16)
    context = jnp.einsum(
        "bkgqns,bnskd->bqkgd", weights, picked_values, preferred_element_type=jnp.float32
    )
    context = context.astype(jnp.bfloat16).reshape(row_count, query_cols)
    share_terms = jnp.dot(
        context, lax.all_gather(wo, "fsdp", axis=1, tiled=True), preferred_element_type=jnp.float32
    )
    return lax.psum_scatter(
        share_terms.astype(jnp.bfloat16), "ctx", scatter_dimension=1, tiled=True
    )


def solution(mesh):
    in_specs = (
        P("fsdp", None),
        P("fsdp", "ctx"),
        P("ctx", "fsdp"),
        P(("fsdp", "ctx"), None),
        P(("fsdp", "ctx"), None),
        P("fsdp", None, None),
    )
    out_specs = P("fsdp", "ctx")
    return jax.shard_map(body, mesh=mesh, in_specs=in_specs, out_specs=out_specs, check_vma=False)
```

profile of v0, /device:TPU:1, one launch (start us, length us, event | category | flops | bytes accessed | tf_op | source)
XLA Modules:
  0.0 360.2 jit_solution(5195303256417563035)
XLA Ops:
  6.5 0.7 all-gather.5.cloned.1.call-update
  7.3 0.7 all-gather.7.cloned.1.call-update
  8.1 0.7 all-gather.9.cloned.1.call-update
  8.8 0.5 all-gather.11.cloned.1.call-update
  9.4 0.7 compare_select_fusion
  10.2 0.8 fusion.28
  11.0 0.5 multiply_cosine_fusion
  11.8 56.0 %all-gather.5.cloned.1.call-done = bf16[2048,1024]{1,0:T(8,128)(2,1)} async-done(((bf16[256,1024]{1,0:T(8,128)(2,1)}), bf16[2048,1024]{1,0:T(8,128)(2,1)}) %all-gather.5.cloned.1.call-update) | async-done | bytes 4194320 | tf_op jit(solution)/shard_map/all_gather | solution.py:46
  67.8 55.2 %all-gather.7.cloned.1.call-done = bf16[2048,1024]{1,0:T(8,128)(2,1)} async-done(((bf16[256,1024]{1,0:T(8,128)(2,1)}), bf16[2048,1024]{1,0:T(8,128)(2,1)}) %all-gather.7.cloned.1.call-update) | async-done | bytes 4194320 | tf_op jit(solution)/shard_map/all_gather | solution.py:45
  123.0 1.3 constant_dynamic-slice_fusion
  124.3 0.7 gather_fusion.1
  125.1 0.7 gather_fusion
  125.8 1.3 copy.8
  127.2 55.4 %all-gather.9.cloned.1.call-done = bf16[8192,512]{1,0:T(8,128)(2,1)} async-done(((bf16[256,512]{1,0:T(8,128)(2,1)}), bf16[8192,512]{1,0:T(8,128)(2,1)}) %all-gather.9.cloned.1.call-update) | async-done | bytes 8388624 | tf_op jit(solution)/shard_map/all_gather | solution.py:35
  182.6 9.4 %fusion.34 = f32[512,512]{0,1:T(8,128)S(1)} fusion(bf16[512,8192]{1,0:T(8,128)(2,1)} %param.8, bf16[8192,512]{1,0:T(8,128)(2,1)} %all-gather.9.cloned.1.call-done), kind=kOutput, calls=%fused_computation.49 | convolution fusion | flops 4294967296 | bytes 17825792 | tf_op jit(solution)/shard_map/dot_general | solution.py:34
  192.0 1.0 multiply_subtract_fusion
  193.5 1.2 concatenate.9
  194.7 1.3 copy.9
  196.0 2.7 fusion
  198.7 1.7 fusion.1
  200.5 2.2 fusion.10
  203.0 46.1 %all-gather.11.cloned.1.call-done = bf16[512,8192]{1,0:T(8,128)(2,1)} async-done(((bf16[512,256]{1,0:T(8,128)(2,1)}), bf16[512,8192]{1,0:T(8,128)(2,1)}) %all-gather.11.cloned.1.call-update) | async-done | bytes 8388624 | tf_op jit(solution)/shard_map/all_gather | solution.py:77
  249.1 10.0 %convolution_convert_fusion = bf16[512,8192]{1,0:T(8,128)(2,1)} fusion(bf16[512,8192]{1,0:T(8,128)(2,1)} %all-gather.11.cloned.1.call-done, bf16[64,8,4,128]{3,2,1,0:T(4,128)(2,1)S(1)} %bitcast.100), kind=kOutput, calls=%fused_computation.2 | convolution fusion | flops 4299161600 | bytes 17301504 | tf_op jit(solution)/shard_map/dot_general | solution.py:76
  259.2 94.5 %reduce-scatter.2.cloned.1.call-done = bf16[512,1024]{1,0:T(8,128)(2,1)} async-done(((bf16[512,8192]{1,0:T(8,128)(2,1)}), bf16[512,1024]{1,0:T(8,128)(2,1)}) %reduce-scatter.2.cloned.1.call-update) | async-done | bytes 1048592 | tf_op jit(solution)/shard_map/reduce_scatter | solution.py:79
  (18 shorter events, 1.4 us)
Async XLA Ops:
  6.5 61.3 %all-gather.5.cloned.1.call-start = ((), (), s32[]{:S(2)}) async-start(), calls=%async_computation.1 | async-start | bytes 4718592 | tf_op jit(solution)/shard_map/all_gather | solution.py:46
  7.3 115.8 %all-gather.7.cloned.1.call-start = ((), (), s32[]{:S(2)}) async-start(), calls=%async_computation.2 | async-start | bytes 4718592 | tf_op jit(solution)/shard_map/all_gather | solution.py:45
  8.0 174.6 %all-gather.9.cloned.1.call-start = ((), (), s32[]{:S(2)}) async-start(), calls=%async_computation.3 | async-start | bytes 8650752 | tf_op jit(solution)/shard_map/all_gather | solution.py:35
  8.7 240.4 %all-gather.11.cloned.1.call-start = ((), (), s32[]{:S(2)}) async-start(), calls=%async_computation.4 | async-start | bytes 8650752 | tf_op jit(solution)/shard_map/all_gather | solution.py:77
  9.3 344.3 %reduce-scatter.2.cloned.1.call-start = ((), (), s32[]{:S(2)}) async-start(), calls=%async_computation.5 | async-start | bytes 9437184 | tf_op jit(solution)/shard_map/reduce_scatter | solution.py:79
  198.7 1.8 copy-start
Sparse Core Ops, SparseCore 0:
  9.1 58.6 all-gather.4
  69.6 53.4 all-gather.6
  125.6 56.9 all-gather.8
  184.9 64.1 all-gather.10
  259.3 94.2 reduce-scatter.1
where the time goes:
time: 360 us
  waiting for transfers between devices  310 us (86%)
  matrix products  24.3 us (7%)
  between operations  13.3 us (4%)
  local copies, waits for them, and re-layouts  7.56 us (2%)
  other arithmetic  5.01 us (1%)
    reduce_scatter x1, waiting for transfers between devices, body(): lax.psum_scatter(share_terms.astype(jnp.bfloat16), 'ctx', scatter_dimensi...  94.5 us
    all_gather x1, waiting for transfers between devices, body(): lax.all_gather(value_cache, 'ctx', axis=0, tiled=True)  56 us
    all_gather x1, waiting for transfers between devices, body(): lax.all_gather(wq, 'fsdp', axis=0, tiled=True)  55.4 us
    all_gather x1, waiting for transfers between devices, body(): lax.all_gather(key_cache, 'ctx', axis=0, tiled=True)  55.2 us
    all_gather x1, waiting for transfers between devices, body(): lax.all_gather(wo, 'fsdp', axis=1, tiled=True)  46.1 us
    dot_general x1, matrix products, body(): jnp.dot(context, lax.all_gather(wo, 'fsdp', axis=1, tiled=True), preferre...  10 us
    dot_general x1, matrix products, body(): jnp.dot(tokens, lax.all_gather(wq, 'fsdp', axis=0, tiled=True), preferred...  9.44 us
  transfers between devices with their start and end apart: 5, of which 5 were waited for; matrix products, arithmetic and copies ran while one was open for 7% of the time, Pallas kernels for 0%

commit v1 on v0

--- a/solution.py
+++ b/solution.py
@@ -6,6 +6,27 @@
 HEAD = 128
 BLOCK = 128
 rope_base = 1000000.0
+
+
+def collect(shard, axis, dim):
+    peers, place, rows = (lax.axis_size(axis), lax.axis_index(axis), shard.shape[dim])
+    forward = [(i, (i + 1) % peers) for i in range(peers)]
+    left = [(i, (i - 1) % peers) for i in range(peers)]
+    result = jnp.zeros((*shard.shape[:dim], peers * rows, *shard.shape[dim + 1 :]), shard.dtype)
+    result = lax.dynamic_update_slice_in_dim(result, shard, place * rows, axis=dim)
+    from_left = from_right = shard
+    half = peers // 2
+    for step in range(1, half + 1):
+        from_left = lax.ppermute(from_left, axis, forward)
+        result = lax.dynamic_update_slice_in_dim(
+            result, from_left, (place - step) % peers * rows, axis=dim
+        )
+        if step < peers - half:
+            from_right = lax.ppermute(from_right, axis, left)
+            result = lax.dynamic_update_slice_in_dim(
+                result, from_right, (place + step) % peers * rows, axis=dim
+            )
+    return result
 
 
 def rotate(vectors, positions):
@@ -42,7 +63,7 @@
     ).astype(jnp.bfloat16)
     kv_cols = key_cache.shape[1] // ctx_count
     keys_whole, values_whole = (
-        lax.all_gather(key_cache, "ctx", axis=0, tiled=True),
+        collect(key_cache, "ctx", 0),
         lax.all_gather(value_cache, "ctx", axis=0, tiled=True),
     )
     first_col = lax.axis_index("ctx") * kv_cols

time: 360 us -> 337 us (0.936)
  waiting for transfers between devices: 310 us -> 263 us
  starting transfers between devices: 0.15 us -> 12.4 us
  local copies, waits for them, and re-layouts: 7.56 us -> 17.9 us
    ppermute x0 -> x7, waiting for transfers between devices: none -> 67 us  [the longest x4 66.4 us: collect(): from_left = lax.ppermute(from_left, axis, forward)]
    all_gather x1, waiting for transfers between devices: 56 us -> 0.01 us  [body(): lax.all_gather(value_cache, 'ctx', axis=0, tiled=True)]
    all_gather x1 -> x0, waiting for transfers between devices: 55.2 us -> none  [body(): lax.all_gather(key_cache, 'ctx', axis=0, tiled=True)]
    ppermute x0 -> x7, starting transfers between devices: none -> 12.3 us  [the longest x3 9.71 us: collect(): from_right = lax.ppermute(from_right, axis, left)]
    dynamic_update_slice x0 -> x8, local copies, waits for them, and re-layouts: none -> 7.8 us  [the longest x4 3.38 us: collect(): lax.dynamic_update_slice_in_dim(result, from_left, (place - step) % peers...]
  transfers between devices with their start and end apart: 5 -> 11, of which waited for: 5 -> 8; matrix products, arithmetic and copies ran while one was open for 7% -> 11% of each run, Pallas kernels for 0% -> 0%
where the time goes in v1:
time: 337 us; the launch traced here: 336 us
  waiting for transfers between devices  263 us (78%)
  matrix products  24.4 us (7%)
  local copies, waits for them, and re-layouts  17.9 us (5%)
  between operations  13.4 us (4%)
  starting transfers between devices  12.4 us (4%)
  other arithmetic  5.01 us (1%)
    reduce_scatter x1, waiting for transfers between devices, body(): lax.psum_scatter(share_terms.astype(jnp.bfloat16), 'ctx', scatter_dimensi...  94.5 us
    ppermute x4, waiting for transfers between devices, collect(): from_left = lax.ppermute(from_left, axis, forward)  66.4 us
    all_gather x1, waiting for transfers between devices, body(): lax.all_gather(wq, 'fsdp', axis=0, tiled=True)  53.6 us
    all_gather x1, waiting for transfers between devices, body(): lax.all_gather(wo, 'fsdp', axis=1, tiled=True)  46.3 us
    dot_general x1, matrix products, body(): jnp.dot(context, lax.all_gather(wo, 'fsdp', axis=1, tiled=True), preferre...  10 us
    ppermute x3, starting transfers between devices, collect(): from_right = lax.ppermute(from_right, axis, left)  9.71 us
    dot_general x1, matrix products, body(): jnp.dot(tokens, lax.all_gather(wq, 'fsdp', axis=0, tiled=True), preferred...  9.44 us
  transfers between devices with their start and end apart: 11, of which 8 were waited for; matrix products, arithmetic and copies ran while one was open for 11% of the time, Pallas kernels for 0%

profile of v1, /device:TPU:1, one launch (start us, length us, event | category | flops | bytes accessed | tf_op | source)
XLA Modules:
  0.0 336.4 jit_solution(6924612069814177868)
XLA Ops:
  8.8 2.5 collective-permute-start
  11.3 4.0 %collective-permute-start.1 = (bf16[256,1024]{1,0:T(8,128)(2,1)}, bf16[256,1024]{1,0:T(8,128)(2,1)S(1)}, u32[]{:S(2)}, u32[]{:S(2)}) collective-permute-start(bf16[256,1024]{1,0:T(8,128)(2,1)} %param.11), channel_id=1, source_target_pairs={{0,7},{1,0},{2,1},{3,2},{4,3},{5,4},{6,5},{7,6},{8,15},{9,8},{10,9... | collective-permute-start | bytes 1572872 | tf_op jit(solution)/shard_map/ppermute | solution.py:25
  16.1 11.1 %collective-permute-done = bf16[256,1024]{1,0:T(8,128)(2,1)S(1)} collective-permute-done((bf16[256,1024]{1,0:T(8,128)(2,1)}, bf16[256,1024]{1,0:T(8,128)(2,1)S(1)}, u32[]{:S(2)}, u32[]{:S(2)}) %collective-permute-start) | collective-permute-done | bytes 524320 | tf_op jit(solution)/shard_map/ppermute | solution.py:20
  28.4 3.0 collective-permute-start.3
  31.5 21.5 %collective-permute-done.2 = bf16[256,1024]{1,0:T(8,128)(2,1)S(1)} collective-permute-done((bf16[256,1024]{1,0:T(8,128)(2,1)S(1)}, bf16[256,1024]{1,0:T(8,128)(2,1)S(1)}, u32[]{:S(2)}, u32[]{:S(2)}) %collective-permute-start.2) | collective-permute-done | bytes 524320 | tf_op jit(solution)/shard_map/ppermute | solution.py:20
  53.2 2.5 broadcast_in_dim.24
  55.7 1.9 constant_dynamic-update-slice_fusion.7
  57.9 2.7 collective-permute-start.5
  60.6 0.9 constant_dynamic-update-slice_fusion.6
  61.4 17.2 %collective-permute-done.4 = bf16[256,1024]{1,0:T(8,128)(2,1)S(1)} collective-permute-done((bf16[256,1024]{1,0:T(8,128)(2,1)S(1)}, bf16[256,1024]{1,0:T(8,128)(2,1)S(1)}, u32[]{:S(2)}, u32[]{:S(2)}) %collective-permute-start.4) | collective-permute-done | bytes 524320 | tf_op jit(solution)/shard_map/ppermute | solution.py:20
  83.4 16.6 %collective-permute-done.6 = bf16[256,1024]{1,0:T(8,128)(2,1)S(1)} collective-permute-done((bf16[256,1024]{1,0:T(8,128)(2,1)S(1)}, bf16[256,1024]{1,0:T(8,128)(2,1)S(1)}, u32[]{:S(2)}, u32[]{:S(2)}) %collective-permute-start.6) | collective-permute-done | bytes 524320 | tf_op jit(solution)/shard_map/ppermute | solution.py:20
  100.9 1.3 constant_dynamic-slice_fusion
  103.7 1.3 copy.8
  105.1 53.6 %all-gather.6.cloned.1.call-done = bf16[8192,512]{1,0:T(8,128)(2,1)} async-done(((bf16[256,512]{1,0:T(8,128)(2,1)}), bf16[8192,512]{1,0:T(8,128)(2,1)}) %all-gather.6.cloned.1.call-update) | async-done | bytes 8388624 | tf_op jit(solution)/shard_map/all_gather | solution.py:56
  158.6 9.4 %fusion.34 = f32[512,512]{0,1:T(8,128)S(1)} fusion(bf16[512,8192]{1,0:T(8,128)(2,1)} %param.8, bf16[8192,512]{1,0:T(8,128)(2,1)} %all-gather.6.cloned.1.call-done), kind=kOutput, calls=%fused_computation.57 | convolution fusion | flops 4294967296 | bytes 17825792 | tf_op jit(solution)/shard_map/dot_general | solution.py:55
  168.1 1.0 multiply_subtract_fusion
  169.6 1.2 concatenate.9
  170.8 1.3 copy.9
  172.1 2.7 fusion
  174.8 1.7 fusion.1
  176.5 2.2 fusion.10
  179.1 46.3 %all-gather.8.cloned.1.call-done = bf16[512,8192]{1,0:T(8,128)(2,1)} async-done(((bf16[512,256]{1,0:T(8,128)(2,1)}), bf16[512,8192]{1,0:T(8,128)(2,1)}) %all-gather.8.cloned.1.call-update) | async-done | bytes 8388624 | tf_op jit(solution)/shard_map/all_gather | solution.py:98
  225.3 10.0 %convolution_convert_fusion = bf16[512,8192]{1,0:T(8,128)(2,1)} fusion(bf16[512,8192]{1,0:T(8,128)(2,1)} %all-gather.8.cloned.1.call-done, bf16[64,8,4,128]{3,2,1,0:T(4,128)(2,1)S(1)} %bitcast.100), kind=kOutput, calls=%fused_computation.2 | convolution fusion | flops 4299161600 | bytes 17301504 | tf_op jit(solution)/shard_map/dot_general | solution.py:97
  235.4 94.5 %reduce-scatter.2.cloned.1.call-done = bf16[512,1024]{1,0:T(8,128)(2,1)} async-done(((bf16[512,8192]{1,0:T(8,128)(2,1)}), bf16[512,1024]{1,0:T(8,128)(2,1)}) %reduce-scatter.2.cloned.1.call-update) | async-done | bytes 1048592 | tf_op jit(solution)/shard_map/reduce_scatter | solution.py:100
  (38 shorter events, 12.6 us)
Async XLA Ops:
  6.5 94.4 %all-gather.4.cloned.1.call-start = ((), (), s32[]{:S(2)}) async-start(), calls=%async_computation.1 | async-start | bytes 4718592 | tf_op jit(solution)/shard_map/all_gather | solution.py:67
  7.3 151.4 %all-gather.6.cloned.1.call-start = ((), (), s32[]{:S(2)}) async-start(), calls=%async_computation.2 | async-start | bytes 8650752 | tf_op jit(solution)/shard_map/all_gather | solution.py:56
  8.0 217.3 %all-gather.8.cloned.1.call-start = ((), (), s32[]{:S(2)}) async-start(), calls=%async_computation.3 | async-start | bytes 8650752 | tf_op jit(solution)/shard_map/all_gather | solution.py:98
  8.7 321.1 %reduce-scatter.2.cloned.1.call-start = ((), (), s32[]{:S(2)}) async-start(), calls=%async_computation.4 | async-start | bytes 9437184 | tf_op jit(solution)/shard_map/reduce_scatter | solution.py:100
  8.8 18.3 %collective-permute-start = (bf16[256,1024]{1,0:T(8,128)(2,1)}, bf16[256,1024]{1,0:T(8,128)(2,1)S(1)}, u32[]{:S(2)}, u32[]{:S(2)}) collective-permute-start(bf16[256,1024]{1,0:T(8,128)(2,1)} %param.11), channel_id=1, source_target_pairs={{0,1},{1,2},{2,3},{3,4},{4,5},{5,6},{6,7},{7,0},{8,9},{9,10},{10,1... | collective-permute-start | bytes 1572872 | tf_op jit(solution)/shard_map/ppermute | solution.py:20
  11.3 17.1 %collective-permute-start.1 = (bf16[256,1024]{1,0:T(8,128)(2,1)}, bf16[256,1024]{1,0:T(8,128)(2,1)S(1)}, u32[]{:S(2)}, u32[]{:S(2)}) collective-permute-start(bf16[256,1024]{1,0:T(8,128)(2,1)} %param.11), channel_id=1, source_target_pairs={{0,7},{1,0},{2,1},{3,2},{4,3},{5,4},{6,5},{7,6},{8,15},{9,8},{10,9... | collective-permute-start | bytes 1572872 | tf_op jit(solution)/shard_map/ppermute | solution.py:25
  27.1 25.9 %collective-permute-start.2 = (bf16[256,1024]{1,0:T(8,128)(2,1)S(1)}, bf16[256,1024]{1,0:T(8,128)(2,1)S(1)}, u32[]{:S(2)}, u32[]{:S(2)}) collective-permute-start(bf16[256,1024]{1,0:T(8,128)(2,1)S(1)} %collective-permute-done), channel_id=1, source_target_pairs={{0,1},{1,2},{2,3},{3,4},{4,5},{5,6},{6,7},{7,0},{8,9},{9,10},{10,1... | collective-permute-start | bytes 1572872 | tf_op jit(solution)/shard_map/ppermute | solution.py:20
  28.4 29.4 %collective-permute-start.3 = (bf16[256,1024]{1,0:T(8,128)(2,1)S(1)}, bf16[256,1024]{1,0:T(8,128)(2,1)S(1)}, u32[]{:S(2)}, u32[]{:S(2)}) collective-permute-start(bf16[256,1024]{1,0:T(8,128)(2,1)S(1)} %collective-permute-done.1), channel_id=1, source_target_pairs={{0,7},{1,0},{2,1},{3,2},{4,3},{5,4},{6,5},{7,6},{8,15},{9,8},{10,9... | collective-permute-start | bytes 1572872 | tf_op jit(solution)/shard_map/ppermute | solution.py:25
  53.0 25.7 %collective-permute-start.4 = (bf16[256,1024]{1,0:T(8,128)(2,1)S(1)}, bf16[256,1024]{1,0:T(8,128)(2,1)S(1)}, u32[]{:S(2)}, u32[]{:S(2)}) collective-permute-start(bf16[256,1024]{1,0:T(8,128)(2,1)S(1)} %collective-permute-done.2), channel_id=1, source_target_pairs={{0,1},{1,2},{2,3},{3,4},{4,5},{5,6},{6,7},{7,0},{8,9},{9,10},{10,1... | collective-permute-start | bytes 1572872 | tf_op jit(solution)/shard_map/ppermute | solution.py:20
  57.9 24.7 %collective-permute-start.5 = (bf16[256,1024]{1,0:T(8,128)(2,1)S(1)}, bf16[256,1024]{1,0:T(8,128)(2,1)S(1)}, u32[]{:S(2)}, u32[]{:S(2)}) collective-permute-start(bf16[256,1024]{1,0:T(8,128)(2,1)S(1)} %collective-permute-done.3), channel_id=1, source_target_pairs={{0,7},{1,0},{2,1},{3,2},{4,3},{5,4},{6,5},{7,6},{8,15},{9,8},{10,9... | collective-permute-start | bytes 1572872 | tf_op jit(solution)/shard_map/ppermute | solution.py:25
  78.7 21.4 %collective-permute-start.6 = (bf16[256,1024]{1,0:T(8,128)(2,1)S(1)}, bf16[256,1024]{1,0:T(8,128)(2,1)S(1)}, u32[]{:S(2)}, u32[]{:S(2)}) collective-permute-start(bf16[256,1024]{1,0:T(8,128)(2,1)S(1)} %collective-permute-done.4), channel_id=1, source_target_pairs={{0,1},{1,2},{2,3},{3,4},{4,5},{5,6},{6,7},{7,0},{8,9},{9,10},{10,1... | collective-permute-start | bytes 1572872 | tf_op jit(solution)/shard_map/ppermute | solution.py:20
  174.8 1.8 copy-start
Sparse Core Ops, SparseCore 0:
  9.1 87.0 all-gather.3
  98.8 59.7 all-gather.5
  161.1 64.1 all-gather.7
  235.5 94.2 reduce-scatter.1
